TPU v7x, 32 devices: a whole 2x2x4 slice. The times are simulated.
32 devices in a mesh: file: 16 (over z, y, core), win: 2 (over x).
Axes of the slice: x: 2, y: 2, z: 4, core: 2. Of those that a mesh axis runs over, the one named last changes fastest.
Arguments:
- raw: bfloat16 [2, 128, 20480], P('win', None, 'file'), may hold values from -60 to 60
- fir_taps: float32 [64], replicated, may hold values from -0.75 to 0.75
- offsets: int32 [2, 16], P('win', 'file'), may hold values from 0 to 9
- vs_index: int32 [64], replicated, may hold values from 0 to 127, as said below
Outputs:
- correlation: float32 [64, 128, 2048], P('win', 'file')
Inputs may be any that keep to these rules, and one draw needn't show every extreme that they name: `vs_index`: virtual source s is one of the channels s * 2 to s * 2 + 1.
All inputs are finite; a program needn't handle non-finite values.
Results may differ from a plain program's by a relative error of at most 0.0063.
Values may be sent and summed in bfloat16 or wider, within the bound.
No kernel may reach another device: no remote copies, remote signals or barrier semaphores. Data moves between devices by JAX's collectives and lax.ppermute only.
A program may use at most 128 MiB of HBM per device.

v0:
```python
import math
import jax
import jax.numpy as jnp
from jax import lax
from jax.sharding import PartitionSpec as P

R = 10
TAPS = 64
TD = 128
SEG = 2048
BAND = 64
VS_DEV = 4
PRECISE = lax.Precision.HIGHEST
EPSILON = 1e-06


def phase_table(height, breadth, period_len):
    row_index = lax.broadcasted_iota(jnp.int32, (height, breadth), 0)
    col_index = lax.broadcasted_iota(jnp.int32, (height, breadth), 1)
    residue = row_index * col_index % period_len
    angles = residue.astype(jnp.float32) * (2.0 * math.pi / period_len)
    return (jnp.cos(angles), jnp.sin(angles))


def forward_spectrum(samples):
    length = samples.shape[-1]
    factor = min(128, length)
    inner = length // factor
    outer = 2 * length // factor
    half_factor = factor // 2
    leading = samples.shape[:-1]
    arranged = samples.astype(jnp.float32).reshape(leading + (inner, factor))
    cos_a, sin_a = phase_table(inner, outer, outer)
    first_re = jnp.einsum("...pa,pm->...ma", arranged, cos_a, precision=PRECISE)
    first_im = -jnp.einsum("...pa,pm->...ma", arranged, sin_a, precision=PRECISE)
    cos_t, sin_t = phase_table(outer, factor, 2 * length)
    twist_re = first_re * cos_t + first_im * sin_t
    twist_im = first_im * cos_t - first_re * sin_t
    cos_b, sin_b = phase_table(factor, half_factor, factor)
    out_re = jnp.einsum("...ma,an->...nm", twist_re, cos_b, precision=PRECISE) + jnp.einsum(
        "...ma,an->...nm", twist_im, sin_b, precision=PRECISE
    )
    out_im = jnp.einsum("...ma,an->...nm", twist_im, cos_b, precision=PRECISE) - jnp.einsum(
        "...ma,an->...nm", twist_re, sin_b, precision=PRECISE
    )
    return (out_re.reshape(leading + (length,)), out_im.reshape(leading + (length,)))


def inverse_lags(cross_re, cross_im):
    length = cross_re.shape[-1]
    factor = min(128, length)
    inner = length // factor
    outer = 2 * length // factor
    half_factor = factor // 2
    leading = cross_re.shape[:-1]
    quarter = jnp.arange(length, dtype=jnp.int32) % 4
    rotate_c = jnp.where(quarter == 0, 1.0, jnp.where(quarter == 2, -1.0, 0.0)).astype(jnp.float32)
    rotate_s = jnp.where(quarter == 1, 1.0, jnp.where(quarter == 3, -1.0, 0.0)).astype(jnp.float32)
    turned_re = (cross_re * rotate_c + cross_im * rotate_s).reshape(leading + (inner, factor))
    turned_im = (cross_im * rotate_c - cross_re * rotate_s).reshape(leading + (inner, factor))
    cos_a, sin_a = phase_table(inner, outer, outer)
    first_re = jnp.einsum("...pa,pm->...ma", turned_re, cos_a, precision=PRECISE) - jnp.einsum(
        "...pa,pm->...ma", turned_im, sin_a, precision=PRECISE
    )
    first_im = jnp.einsum("...pa,pm->...ma", turned_re, sin_a, precision=PRECISE) + jnp.einsum(
        "...pa,pm->...ma", turned_im, cos_a, precision=PRECISE
    )
    cos_t, sin_t = phase_table(outer, factor, 2 * length)
    twist_re = first_re * cos_t - first_im * sin_t
    twist_im = first_re * sin_t + first_im * cos_t
    cos_b, sin_b = phase_table(factor, half_factor, factor)
    lagged = jnp.einsum("...ma,an->...nm", twist_re, cos_b, precision=PRECISE) - jnp.einsum(
        "...ma,an->...nm", twist_im, sin_b, precision=PRECISE
    )
    return lagged.reshape(leading + (length,))


def whiten(spec_re, spec_im):
    length = spec_re.shape[-1]
    leading = spec_re.shape[:-1]
    magnitude = jnp.sqrt(spec_re * spec_re + spec_im * spec_im)
    amplitude = (
        jnp.mean(magnitude.reshape(leading + (length // BAND, BAND)), axis=-1, keepdims=True)
        + EPSILON
    )
    white_re = (spec_re.reshape(leading + (length // BAND, BAND)) / amplitude).reshape(
        leading + (length,)
    )
    white_im = (spec_im.reshape(leading + (length // BAND, BAND)) / amplitude).reshape(
        leading + (length,)
    )
    return (white_re.astype(jnp.bfloat16), white_im.astype(jnp.bfloat16))


def band_matrix(fir_taps, block_width):
    span = R * block_width + TAPS - R
    period_len = span + R
    flipped = fir_taps[::-1].astype(jnp.bfloat16)
    pattern = jnp.concatenate([flipped, jnp.zeros((period_len - TAPS,), jnp.bfloat16)])
    flat = jnp.tile(pattern, block_width)[: block_width * span]
    return flat.reshape(block_width, span).T


def decimate(extended, offset_now, band_taps):
    row_count = extended.shape[0]
    block_width = band_taps.shape[1]
    span = R * (TD - 1) + TAPS
    segment = lax.dynamic_slice_in_dim(extended, offset_now + 1, span, axis=1)
    block_count = TD // block_width
    stride_len = R * block_width
    leading_part = segment[:, : stride_len * block_count].reshape(
        row_count, block_count, stride_len
    )
    trailing = segment[:, stride_len:]
    trailing = jnp.pad(trailing, ((0, 0), (0, stride_len * block_count - trailing.shape[1])))
    trailing = trailing.reshape(row_count, block_count, stride_len)[:, :, : TAPS - R]
    blocks = jnp.concatenate([leading_part, trailing], axis=2)
    result = jnp.einsum("cbi,io->cbo", blocks, band_taps, preferred_element_type=jnp.float32)
    return result.reshape(row_count, TD)


def local(raw, fir_taps, offsets, vs_index):
    samples = raw[0]
    file_count = lax.axis_size("file")
    win_count = lax.axis_size("win")
    band_taps = band_matrix(fir_taps, math.gcd(TD, 128))
    regrouped = lax.all_to_all(samples, "file", split_axis=0, concat_axis=1, tiled=True)
    shifts = lax.all_gather(offsets, "file", axis=1, tiled=True)
    row_count = regrouped.shape[0]
    file_blocks = regrouped.reshape(row_count, file_count, regrouped.shape[1] // file_count)
    previous = jnp.concatenate(
        [
            jnp.zeros((row_count, 1, TAPS), file_blocks.dtype),
            file_blocks[:, :-1, file_blocks.shape[2] - TAPS :],
        ],
        axis=1,
    )
    extended = jnp.concatenate([previous, file_blocks], axis=2)
    pieces = jax.vmap(decimate, in_axes=(1, 0, None), out_axes=1)(extended, shifts[0], band_taps)
    owned = pieces.reshape(row_count, file_count * TD).astype(jnp.bfloat16)
    row_count = owned.shape[0]
    seg_count = owned.shape[1] // SEG
    own_re, own_im = forward_spectrum(owned.reshape(row_count, seg_count, SEG))
    white_re, white_im = whiten(own_re, own_im)
    file_pos = lax.axis_index("file")
    source_rows = (
        lax.dynamic_slice_in_dim(vs_index, file_pos * VS_DEV, VS_DEV) - file_pos * row_count
    )
    source_re, source_im = (
        lax.all_gather(jnp.take(white_re, source_rows, axis=0), "file", axis=0, tiled=True),
        lax.all_gather(jnp.take(white_im, source_rows, axis=0), "file", axis=0, tiled=True),
    )
    own_both = jnp.concatenate([white_re, white_im], axis=1)
    scale_out = 1.0 / math.sqrt(SEG * seg_count * win_count)
    paired = jnp.stack(
        [
            jnp.concatenate([source_re, source_im], axis=1),
            jnp.concatenate([-source_im, source_re], axis=1),
        ],
        axis=1,
    )
    joined = jnp.einsum("cqf,sdqf->scdf", own_both, paired, preferred_element_type=jnp.float32)
    stacked = lax.psum_scatter(
        joined.reshape(joined.shape[0], joined.shape[1], 2 * SEG),
        "win",
        scatter_dimension=0,
        tiled=True,
    )
    return inverse_lags(stacked[..., :SEG], stacked[..., SEG:]) * scale_out


def solution(mesh):
    return jax.shard_map(
        local,
        mesh=mesh,
        in_specs=(P("win", None, "file"), P(), P("win", "file"), P()),
        out_specs=P("win", "file", None),
        check_vma=False,
    )
```

profile of v0, /device:TPU:0, one launch (start us, length us, event | category | flops | bytes accessed | tf_op | source)
XLA Modules:
  0.0 293.7 jit_solution(40036436673634234)
XLA Ops:
  6.5 7.4 %all-to-all-start = ((bf16[16,8,1280]{2,1,0:T(8,128)(2,1)}), bf16[16,8,1280]{2,1,0:T(8,128)(2,1)S(1)}, u32[]{:S(2)}, u32[]{:S(2)}) async-start(bf16[16,8,1280]{2,1,0:T(8,128)(2,1)} %bitcast.144), calls=%async_computation | async-start | bytes 655360 | tf_op jit(solution)/shard_map/all_to_all | solution.py:127
  17.3 12.4 %all-reduce.4 = s32[16]{0:T(128)S(1)} all-reduce(s32[16]{0:T(128)S(1)} %bitcast_dynamic-update-slice_fusion), channel_id=1, replica_groups=mesh['file'=16,'win'=2] {'file'}, use_global_device_ids=true, to_apply=%add.4 | all-reduce | flops 16 | bytes 128
  31.9 29.9 %while.1 = (s32[]{:T(128)}, bf16[16,8,1344]{2,1,0:T(8,128)(2,1)S(1)}, s32[16,3]{0,1:T(4,128)S(1)}, bf16[16,8,1334]{2,1,0:T(8,128)(2,1)S(1)}, s32[]{:T(128)}) while((s32[]{:T(128)}, bf16[16,8,1344]{2,1,0:T(8,128)(2,1)S(1)}, s32[16,3]{0,1:T(4,128)S(1)}, bf16[16,8,1334]{2,1,0:T(8,128)(2,1)S(1)}, s32[]{:T(128)}) %tuple.29), condition=%wide.while_cond, body=%wide.while_body.sunk | while | flops 2 | bytes 45173 | solution.py:108
  32.5 1.3 dynamic-slice_dynamic-update-slice_fusion.2
  34.4 1.3 dynamic-slice_dynamic-update-slice_fusion.2
  36.3 1.3 dynamic-slice_dynamic-update-slice_fusion.2
  38.1 1.3 dynamic-slice_dynamic-update-slice_fusion.2
  40.0 1.3 dynamic-slice_dynamic-update-slice_fusion.2
  41.9 1.3 dynamic-slice_dynamic-update-slice_fusion.2
  43.7 1.3 dynamic-slice_dynamic-update-slice_fusion.2
  45.6 1.3 dynamic-slice_dynamic-update-slice_fusion.2
  47.5 1.3 dynamic-slice_dynamic-update-slice_fusion.2
  49.4 1.3 dynamic-slice_dynamic-update-slice_fusion.2
  51.2 1.3 dynamic-slice_dynamic-update-slice_fusion.2
  53.1 1.3 dynamic-slice_dynamic-update-slice_fusion.2
  55.0 1.3 dynamic-slice_dynamic-update-slice_fusion.2
  67.5 19.4 %all_gather.11 = bf16[64,1,2048]{2,1,0:T(2,128)(2,1)S(1)} all-gather(bf16[4,1,2048]{2,1,0:T(2,128)(2,1)S(1)} %copy.77), channel_id=1, replica_groups=mesh['file'=16,'win'=2] {'file'}, dimensions={0}, use_global_device_ids=true | all-gather | bytes 278528 | tf_op jit(solution)/shard_map/all_gather | solution.py:151
  87.1 19.7 %all_gather.10 = bf16[64,1,2048]{2,1,0:T(2,128)(2,1)S(1)} all-gather(bf16[4,1,2048]{2,1,0:T(2,128)(2,1)S(1)} %copy.75), channel_id=1, replica_groups=mesh['file'=16,'win'=2] {'file'}, dimensions={0}, use_global_device_ids=true | all-gather | bytes 278528 | tf_op jit(solution)/shard_map/all_gather | solution.py:150
  108.2 4.5 %copy.82 = bf16[64,2,2,2048]{0,2,1,3:T(2,128)(2,1)S(1)} copy(bf16[64,2,2,2048]{3,0,2,1:T(8,128)(2,1)} %pad_maximum_fusion) | data formatting | bytes 2097152 | tf_op jit(solution)/shard_map/stack | solution.py:155
  112.7 6.9 %convolution_bitcast_fusion = f32[64,8,2,2048]{0,1,2,3:T(8,128)} fusion(bf16[64,2,2,2048]{0,2,1,3:T(2,128)(2,1)S(1)} %copy.82, bf16[8,2,2048,1]{0,1,3,2:T(2,128)(2,1)S(1)} %copy.91), kind=kOutput, calls=%fused_computation.4 | convolution fusion | flops 8388608 | bytes 9502720 | tf_op jit(solution)/shard_map/cqf,sdqf->scdf/dot_general | solution.py:162
  119.6 17.3 %copy.84 = f32[64,8,2,2048]{3,2,1,0:T(2,128)} copy(f32[64,8,2,2048]{0,1,2,3:T(8,128)} %convolution_bitcast_fusion) | data formatting | bytes 16777216 | tf_op jit(solution)/shard_map/cqf,sdqf->scdf/transpose | solution.py:162
  136.8 11.8 %reshape.235 = f32[64,8,4096]{2,1,0:T(8,128)} reshape(f32[64,8,2,2048]{3,2,1,0:T(2,128)} %copy.84) | data formatting | bytes 16777216 | tf_op jit(solution)/shard_map/reshape | solution.py:164
  148.7 97.1 %reduce-scatter.2.cloned.1.call-done = f32[32,8,4096]{2,1,0:T(8,128)} async-done(((f32[64,8,4096]{2,1,0:T(8,128)}), f32[32,8,4096]{2,1,0:T(8,128)}) %reduce-scatter.2.cloned.1.call-update) | async-done | bytes 4194320 | tf_op jit(solution)/shard_map/reduce_scatter | solution.py:163
  245.8 2.8 subtract_bitcast_fusion
  248.6 3.5 %fusion.20 = f32[32,32,8,128]{3,0,2,1:T(8,128)S(1)} fusion(f32[32,8,16,128]{3,1,2,0:T(8,128)S(1)} %get-tuple-element.29), kind=kOutput, calls=%fused_computation.28 | convolution fusion | flops 201333760 | bytes 6291456 | tf_op jit(solution)/shard_map/...pa,pm->...ma/dot_general | solution.py:62
  252.1 3.7 %fusion.18 = f32[32,32,8,128]{3,0,2,1:T(8,128)S(1)} fusion(f32[32,8,16,128]{3,1,2,0:T(8,128)S(1)} %get-tuple-element.29), kind=kOutput, calls=%fused_computation.26 | convolution fusion | flops 201333760 | bytes 6291456 | tf_op jit(solution)/shard_map/...pa,pm->...ma/dot_general | solution.py:65
  255.8 3.6 %convolution_subtract_fusion = f32[32,32,8,128]{3,0,2,1:T(8,128)S(1)} fusion(f32[32,32,8,128]{3,0,2,1:T(8,128)S(1)} %fusion.20, f32[32,8,16,128]{3,1,2,0:T(8,128)S(1)} %get-tuple-element.28), kind=kOutput, calls=%fused_computation.17 | convolution fusion | flops 202382336 | bytes 10485760 | tf_op jit(solution)/shard_map/...pa,pm->...ma/dot_general | solution.py:62
  259.4 4.2 %convolution_add_fusion = f32[32,32,8,128]{3,0,2,1:T(8,128)S(1)} fusion(f32[32,32,8,128]{3,0,2,1:T(8,128)S(1)} %fusion.18, f32[32,8,16,128]{3,1,2,0:T(8,128)S(1)} %get-tuple-element.28), kind=kOutput, calls=%fused_computation.16 | convolution fusion | flops 202382336 | bytes 10485760 | tf_op jit(solution)/shard_map/...pa,pm->...ma/dot_general | solution.py:65
  263.6 3.5 %fusion = f32[64,32,8,32]{0,3,2,1:T(8,128)S(1)} fusion(f32[32,32,8,128]{3,0,2,1:T(8,128)S(1)} %convolution_add_fusion, f32[32,32,8,128]{3,0,2,1:T(8,128)S(1)} %convolution_subtract_fusion, f32[32,128]{1,0:T(8,128)S(1)} %get-tuple-element.38, f32[32,128]{1,0:T(8,128)S(1)} %get-tuple-element.39), kind=kOutput, calls=%fused_computation.5 | convolution fusion | flops 808566784 | bytes 10518528 | tf_op jit(solution)/shard_map/...ma,an->...nm/dot_general | solution.py:72
  267.1 5.3 %multiply_bitcast_fusion = f32[32,8,64,32]{2,3,1,0:T(8,128)} fusion(f32[64,32,8,32]{0,3,2,1:T(8,128)S(1)} %fusion, f32[32,32,8,128]{3,0,2,1:T(8,128)S(1)} %convolution_add_fusion, f32[32,32,8,128]{3,0,2,1:T(8,128)S(1)} %convolution_subtract_fusion, f32[32,128]{1,0:T(8,128)S(1)} %get-tuple-element.38, f32[32,128]{1,0:T(8,128)S(1)} %get-tuple-element.39), kind=kOutput, calls=%fused_computation.9 | convolution fusion | flops 809615360 | bytes 12615680 | tf_op jit(solution)/shard_map/...ma,an->...nm/dot_general | solution.py:72
  272.4 6.9 %copy.89 = f32[32,8,64,32]{3,2,1,0:T(8,128)} copy(f32[32,8,64,32]{2,3,1,0:T(8,128)} %multiply_bitcast_fusion) | data formatting | bytes 4194304 | tf_op jit(solution)/shard_map/mul | solution.py:169
  279.3 7.5 %mul.267 = f32[32,8,2048]{2,1,0:T(8,128)} reshape(f32[32,8,64,32]{3,2,1,0:T(8,128)} %copy.89) | data formatting | bytes 4194304 | tf_op jit(solution)/shard_map/mul | solution.py:169
  (90 shorter events, 25.4 us)
Async XLA Ops:
  6.5 25.1 %all-to-all-start = ((bf16[16,8,1280]{2,1,0:T(8,128)(2,1)}), bf16[16,8,1280]{2,1,0:T(8,128)(2,1)S(1)}, u32[]{:S(2)}, u32[]{:S(2)}) async-start(bf16[16,8,1280]{2,1,0:T(8,128)(2,1)} %bitcast.144), calls=%async_computation | async-start | bytes 655360 | tf_op jit(solution)/shard_map/all_to_all | solution.py:127
  13.9 231.8 %reduce-scatter.2.cloned.1.call-start = ((), (), s32[]{:S(2)}) async-start(), calls=%async_computation.2 | async-start | bytes 12582912 | tf_op jit(solution)/shard_map/reduce_scatter | solution.py:163
Sparse Core Ops, SparseCore 0:
  148.8 96.9 reduce-scatter.1
where the time goes:
time: 295 us; the launch traced here: 294 us
  waiting for transfers between devices  97.1 us (33%)
  local copies, waits for them, and re-layouts  84.7 us (29%)
  blocking collectives  51.5 us (17%)
  matrix products  33.2 us (11%)
  between operations  14.4 us (5%)
  starting transfers between devices  7.43 us (3%)
  other arithmetic  5.31 us (2%)
    reduce_scatter x1, waiting for transfers between devices, local(): lax.psum_scatter(joined.reshape(joined.shape[0], joined.shape[1], 2 * SEG...  97.1 us
    gather x48, local copies, waits for them, and re-layouts  29.9 us
    all_gather x1, blocking collectives, local(): lax.all_gather(jnp.take(white_re, source_rows, axis=0), 'file', axis=0, t...  19.7 us
    all_gather x1, blocking collectives, local(): lax.all_gather(jnp.take(white_im, source_rows, axis=0), 'file', axis=0, t...  19.4 us
    transpose x1, local copies, waits for them, and re-layouts, local(): jnp.einsum('cqf,sdqf->scdf', own_both, paired, preferred_element_type=jnp...  17.3 us
    mul x2, local copies, waits for them, and re-layouts, local(): return inverse_lags(stacked[..., :SEG], stacked[..., SEG:]) * scale_out  14.4 us
    unnamed x1, blocking collectives  12.4 us
    reshape x1, local copies, waits for them, and re-layouts, local(): joined.reshape(joined.shape[0], joined.shape[1], 2 * SEG)  11.8 us
  transfers between devices with their start and end apart: 2, of which 1 were waited for; matrix products, arithmetic and copies ran while one was open for 2% of the time, Pallas kernels for 0%

commit v1 on v0

--- a/solution.py
+++ b/solution.py
@@ -12,6 +12,30 @@
 VS_DEV = 4
 PRECISE = lax.Precision.HIGHEST
 EPSILON = 1e-06
+
+
+def split_up(shard, dim, size):
+    before, after = (shard.shape[:dim], shard.shape[dim + 1 :])
+    return jnp.moveaxis(shard.reshape(*before, size, -1, *after), dim, 0)
+
+
+def laid_out(blocks, dim):
+    shape = list(blocks.shape[1:])
+    shape[dim] *= blocks.shape[0]
+    return jnp.moveaxis(blocks, 0, dim).reshape(shape)
+
+
+def sent_to_each(x, axis, split_dim, concat_dim):
+    devices, index = (lax.axis_size(axis), lax.axis_index(axis))
+    pieces = split_up(x, split_dim, devices)
+    finished = [pieces[index]]
+    for step in range(1, devices):
+        sent = pieces[(index + step) % devices]
+        finished.append(
+            lax.ppermute(sent, axis, [(i, (i + step) % devices) for i in range(devices)])
+        )
+    pieces = jnp.stack(finished)[(index - jnp.arange(devices)) % devices]
+    return laid_out(pieces, concat_dim)
 
 
 def phase_table(height, breadth, period_len):
@@ -124,7 +148,7 @@
     file_count = lax.axis_size("file")
     win_count = lax.axis_size("win")
     band_taps = band_matrix(fir_taps, math.gcd(TD, 128))
-    regrouped = lax.all_to_all(samples, "file", split_axis=0, concat_axis=1, tiled=True)
+    regrouped = sent_to_each(samples, "file", 0, 1)
     shifts = lax.all_gather(offsets, "file", axis=1, tiled=True)
     row_count = regrouped.shape[0]
     file_blocks = regrouped.reshape(row_count, file_count, regrouped.shape[1] // file_count)

time: 295 us -> 320 us (1.085)
  starting transfers between devices: 7.43 us -> 21.2 us
  local copies, waits for them, and re-layouts: 84.7 us -> 90.8 us
    ppermute x0 -> x15, starting transfers between devices: none -> 21.2 us  [sent_to_each(): lax.ppermute(sent, axis, [(i, (i + step) % devices) for i in range(device...]
    all_to_all x1 -> x0, starting transfers between devices: 7.39 us -> none  [local(): lax.all_to_all(samples, 'file', split_axis=0, concat_axis=1, tiled=True)]
    gather x48 -> x49, local copies, waits for them, and re-layouts: 29.9 us -> 34.8 us
    all_gather x1, blocking collectives: 19.4 us -> 23 us  [local(): lax.all_gather(jnp.take(white_im, source_rows, axis=0), 'file', axis=0, t...]
  transfers between devices with their start and end apart: 2 -> 16, of which waited for: 1 -> 3; matrix products, arithmetic and copies ran while one was open for 2% -> 1% of each run, Pallas kernels for 0% -> 0%
where the time goes in v1:
time: 320 us; the launch traced here: 318 us
  waiting for transfers between devices  99.3 us (31%)
  local copies, waits for them, and re-layouts  90.8 us (28%)
  blocking collectives  54 us (17%)
  matrix products  33.2 us (10%)
  starting transfers between devices  21.2 us (7%)
  between operations  14.5 us (5%)
  other arithmetic  5.33 us (2%)
    reduce_scatter x1, waiting for transfers between devices, local(): lax.psum_scatter(joined.reshape(joined.shape[0], joined.shape[1], 2 * SEG...  97.8 us
    gather x48, local copies, waits for them, and re-layouts  34.2 us
    all_gather x1, blocking collectives, local(): lax.all_gather(jnp.take(white_im, source_rows, axis=0), 'file', axis=0, t...  23 us
    ppermute x15, starting transfers between devices, sent_to_each(): lax.ppermute(sent, axis, [(i, (i + step) % devices) for i in range(device...  21.2 us
    all_gather x1, blocking collectives, local(): lax.all_gather(jnp.take(white_re, source_rows, axis=0), 'file', axis=0, t...  18.9 us
    transpose x1, local copies, waits for them, and re-layouts, local(): jnp.einsum('cqf,sdqf->scdf', own_both, paired, preferred_element_type=jnp...  17.3 us
    mul x2, local copies, waits for them, and re-layouts, local(): return inverse_lags(stacked[..., :SEG], stacked[..., SEG:]) * scale_out  14.4 us
    unnamed x1, blocking collectives  12 us
  transfers between devices with their start and end apart: 16, of which 3 were waited for; matrix products, arithmetic and copies ran while one was open for 1% of the time, Pallas kernels for 0%

profile of v1, /device:TPU:0, one launch (start us, length us, event | category | flops | bytes accessed | tf_op | source)
XLA Modules:
  0.0 318.2 jit_solution(4495471105605138776)
XLA Ops:
  8.0 2.6 collective-permute-start.1
  10.6 2.4 collective-permute-start.2
  13.0 1.6 collective-permute-start.3
  17.6 12.0 %all-reduce.4 = s32[16]{0:T(128)S(1)} all-reduce(s32[16]{0:T(128)S(1)} %bitcast_dynamic-update-slice_fusion), channel_id=1, replica_groups=mesh['file'=16,'win'=2] {'file'}, use_global_device_ids=true, to_apply=%add.4 | all-reduce | flops 16 | bytes 128
  34.2 2.3 collective-permute-start.8
  36.5 3.3 %collective-permute-start.9 = (bf16[8,1280]{1,0:T(8,128)(2,1)S(1)}, bf16[8,1280]{1,0:T(8,128)(2,1)S(1)}, u32[]{:S(2)}, u32[]{:S(2)}) collective-permute-start(bf16[8,1280]{1,0:T(8,128)(2,1)S(1)} %get-tuple-element.35), channel_id=1, source_target_pairs={{0,20},{2,22},{4,24},{6,26},{8,28},{10,30},{12,0},{14,2},{16,4},{1... | collective-permute-start | bytes 61448 | tf_op jit(solution)/shard_map/ppermute | solution.py:35
  40.4 1.8 collective-permute-start.11
  42.7 2.3 collective-permute-start.13
  48.6 34.2 %while.1 = (s32[]{:T(128)}, bf16[16,8,1344]{2,1,0:T(8,128)(2,1)S(1)}, s32[16,3]{0,1:T(4,128)S(1)}, bf16[16,8,1334]{2,1,0:T(8,128)(2,1)S(1)}, s32[]{:T(128)}) while((s32[]{:T(128)}, bf16[16,8,1344]{2,1,0:T(8,128)(2,1)S(1)}, s32[16,3]{0,1:T(4,128)S(1)}, bf16[16,8,1334]{2,1,0:T(8,128)(2,1)S(1)}, s32[]{:T(128)}) %tuple.44), condition=%wide.while_cond, body=%wide.while_body.sunk | while | flops 2 | bytes 45173 | solution.py:132
  49.2 1.5 dynamic-slice_dynamic-update-slice_fusion.2
  51.4 1.5 dynamic-slice_dynamic-update-slice_fusion.2
  53.5 1.5 dynamic-slice_dynamic-update-slice_fusion.2
  55.7 1.5 dynamic-slice_dynamic-update-slice_fusion.2
  57.8 1.5 dynamic-slice_dynamic-update-slice_fusion.2
  66.3 1.5 dynamic-slice_dynamic-update-slice_fusion.2
  74.9 1.5 dynamic-slice_dynamic-update-slice_fusion.2
  88.5 23.0 %all_gather.11 = bf16[64,1,2048]{2,1,0:T(2,128)(2,1)S(1)} all-gather(bf16[4,1,2048]{2,1,0:T(2,128)(2,1)S(1)} %copy.77), channel_id=1, replica_groups=mesh['file'=16,'win'=2] {'file'}, dimensions={0}, use_global_device_ids=true | all-gather | bytes 278528 | tf_op jit(solution)/shard_map/all_gather | solution.py:175
  111.7 18.9 %all_gather.10 = bf16[64,1,2048]{2,1,0:T(2,128)(2,1)S(1)} all-gather(bf16[4,1,2048]{2,1,0:T(2,128)(2,1)S(1)} %copy.75), channel_id=1, replica_groups=mesh['file'=16,'win'=2] {'file'}, dimensions={0}, use_global_device_ids=true | all-gather | bytes 278528 | tf_op jit(solution)/shard_map/all_gather | solution.py:174
  131.9 4.5 %copy.82 = bf16[64,2,2,2048]{0,2,1,3:T(2,128)(2,1)S(1)} copy(bf16[64,2,2,2048]{3,0,2,1:T(8,128)(2,1)} %pad_maximum_fusion) | data formatting | bytes 2097152 | tf_op jit(solution)/shard_map/stack | solution.py:179
  136.5 6.9 %convolution_bitcast_fusion = f32[64,8,2,2048]{0,1,2,3:T(8,128)} fusion(bf16[64,2,2,2048]{0,2,1,3:T(2,128)(2,1)S(1)} %copy.82, bf16[8,2,2048,1]{0,1,3,2:T(2,128)(2,1)S(1)} %copy.91), kind=kOutput, calls=%fused_computation.5 | convolution fusion | flops 8388608 | bytes 9502720 | tf_op jit(solution)/shard_map/cqf,sdqf->scdf/dot_general | solution.py:186
  143.3 17.3 %copy.84 = f32[64,8,2,2048]{3,2,1,0:T(2,128)} copy(f32[64,8,2,2048]{0,1,2,3:T(8,128)} %convolution_bitcast_fusion) | data formatting | bytes 16777216 | tf_op jit(solution)/shard_map/cqf,sdqf->scdf/transpose | solution.py:186
  160.6 11.8 %reshape.278 = f32[64,8,4096]{2,1,0:T(8,128)} reshape(f32[64,8,2,2048]{3,2,1,0:T(2,128)} %copy.84) | data formatting | bytes 16777216 | tf_op jit(solution)/shard_map/reshape | solution.py:188
  172.5 97.8 %reduce-scatter.2.cloned.1.call-done = f32[32,8,4096]{2,1,0:T(8,128)} async-done(((f32[64,8,4096]{2,1,0:T(8,128)}), f32[32,8,4096]{2,1,0:T(8,128)}) %reduce-scatter.2.cloned.1.call-update) | async-done | bytes 4194320 | tf_op jit(solution)/shard_map/reduce_scatter | solution.py:187
  270.3 2.8 subtract_bitcast_fusion
  273.1 3.5 %fusion.20 = f32[32,32,8,128]{3,0,2,1:T(8,128)S(1)} fusion(f32[32,8,16,128]{3,1,2,0:T(8,128)S(1)} %get-tuple-element.29), kind=kOutput, calls=%fused_computation.29 | convolution fusion | flops 201333760 | bytes 6291456 | tf_op jit(solution)/shard_map/...pa,pm->...ma/dot_general | solution.py:86
  276.7 3.7 %fusion.18 = f32[32,32,8,128]{3,0,2,1:T(8,128)S(1)} fusion(f32[32,8,16,128]{3,1,2,0:T(8,128)S(1)} %get-tuple-element.29), kind=kOutput, calls=%fused_computation.27 | convolution fusion | flops 201333760 | bytes 6291456 | tf_op jit(solution)/shard_map/...pa,pm->...ma/dot_general | solution.py:89
  280.4 3.6 %convolution_subtract_fusion = f32[32,32,8,128]{3,0,2,1:T(8,128)S(1)} fusion(f32[32,32,8,128]{3,0,2,1:T(8,128)S(1)} %fusion.20, f32[32,8,16,128]{3,1,2,0:T(8,128)S(1)} %get-tuple-element.28), kind=kOutput, calls=%fused_computation.18 | convolution fusion | flops 202382336 | bytes 10485760 | tf_op jit(solution)/shard_map/...pa,pm->...ma/dot_general | solution.py:86
  283.9 4.2 %convolution_add_fusion = f32[32,32,8,128]{3,0,2,1:T(8,128)S(1)} fusion(f32[32,32,8,128]{3,0,2,1:T(8,128)S(1)} %fusion.18, f32[32,8,16,128]{3,1,2,0:T(8,128)S(1)} %get-tuple-element.28), kind=kOutput, calls=%fused_computation.17 | convolution fusion | flops 202382336 | bytes 10485760 | tf_op jit(solution)/shard_map/...pa,pm->...ma/dot_general | solution.py:89
  288.1 3.5 %fusion = f32[64,32,8,32]{0,3,2,1:T(8,128)S(1)} fusion(f32[32,32,8,128]{3,0,2,1:T(8,128)S(1)} %convolution_add_fusion, f32[32,32,8,128]{3,0,2,1:T(8,128)S(1)} %convolution_subtract_fusion, f32[32,128]{1,0:T(8,128)S(1)} %get-tuple-element.54, f32[32,128]{1,0:T(8,128)S(1)} %get-tuple-element.55), kind=kOutput, calls=%fused_computation.6 | convolution fusion | flops 808566784 | bytes 10518528 | tf_op jit(solution)/shard_map/...ma,an->...nm/dot_general | solution.py:96
  291.7 5.3 %multiply_bitcast_fusion = f32[32,8,64,32]{2,3,1,0:T(8,128)} fusion(f32[64,32,8,32]{0,3,2,1:T(8,128)S(1)} %fusion, f32[32,32,8,128]{3,0,2,1:T(8,128)S(1)} %convolution_add_fusion, f32[32,32,8,128]{3,0,2,1:T(8,128)S(1)} %convolution_subtract_fusion, f32[32,128]{1,0:T(8,128)S(1)} %get-tuple-element.54, f32[32,128]{1,0:T(8,128)S(1)} %get-tuple-element.55), kind=kOutput, calls=%fused_computation.10 | convolution fusion | flops 809615360 | bytes 12615680 | tf_op jit(solution)/shard_map/...ma,an->...nm/dot_general | solution.py:96
  296.9 7.0 %copy.89 = f32[32,8,64,32]{3,2,1,0:T(8,128)} copy(f32[32,8,64,32]{2,3,1,0:T(8,128)} %multiply_bitcast_fusion) | data formatting | bytes 4194304 | tf_op jit(solution)/shard_map/mul | solution.py:193
  303.9 7.5 %mul.267 = f32[32,8,2048]{2,1,0:T(8,128)} reshape(f32[32,8,64,32]{3,2,1,0:T(8,128)} %copy.89) | data formatting | bytes 4194304 | tf_op jit(solution)/shard_map/mul | solution.py:193
  (137 shorter events, 43.9 us)
Async XLA Ops:
  6.5 263.8 %reduce-scatter.2.cloned.1.call-start = ((), (), s32[]{:S(2)}) async-start(), calls=%async_computation.1 | async-start | bytes 12582912 | tf_op jit(solution)/shard_map/reduce_scatter | solution.py:187
  7.5 24.7 %collective-permute-start = (bf16[8,1280]{1,0:T(8,128)(2,1)S(1)}, bf16[8,1280]{1,0:T(8,128)(2,1)S(1)}, u32[]{:S(2)}, u32[]{:S(2)}) collective-permute-start(bf16[8,1280]{1,0:T(8,128)(2,1)S(1)} %get-tuple-element.44), channel_id=1, source_target_pairs={{0,2},{2,4},{4,6},{6,8},{8,10},{10,12},{12,14},{14,16},{16,18},{18... | collective-permute-start | bytes 61448 | tf_op jit(solution)/shard_map/ppermute | solution.py:35
  8.0 25.6 %collective-permute-start.1 = (bf16[8,1280]{1,0:T(8,128)(2,1)S(1)}, bf16[8,1280]{1,0:T(8,128)(2,1)S(1)}, u32[]{:S(2)}, u32[]{:S(2)}) collective-permute-start(bf16[8,1280]{1,0:T(8,128)(2,1)S(1)} %get-tuple-element.43), channel_id=1, source_target_pairs={{0,4},{2,6},{4,8},{6,10},{8,12},{10,14},{12,16},{14,18},{16,20},{1... | collective-permute-start | bytes 61448 | tf_op jit(solution)/shard_map/ppermute | solution.py:35
  10.6 23.0 %collective-permute-start.2 = (bf16[8,1280]{1,0:T(8,128)(2,1)S(1)}, bf16[8,1280]{1,0:T(8,128)(2,1)S(1)}, u32[]{:S(2)}, u32[]{:S(2)}) collective-permute-start(bf16[8,1280]{1,0:T(8,128)(2,1)S(1)} %get-tuple-element.42), channel_id=1, source_target_pairs={{0,6},{2,8},{4,10},{6,12},{8,14},{10,16},{12,18},{14,20},{16,22},{... | collective-permute-start | bytes 61448 | tf_op jit(solution)/shard_map/ppermute | solution.py:35
  13.0 21.2 %collective-permute-start.3 = (bf16[8,1280]{1,0:T(8,128)(2,1)S(1)}, bf16[8,1280]{1,0:T(8,128)(2,1)S(1)}, u32[]{:S(2)}, u32[]{:S(2)}) collective-permute-start(bf16[8,1280]{1,0:T(8,128)(2,1)S(1)} %get-tuple-element.41), channel_id=1, source_target_pairs={{0,8},{2,10},{4,12},{6,14},{8,16},{10,18},{12,20},{14,22},{16,24},... | collective-permute-start | bytes 61448 | tf_op jit(solution)/shard_map/ppermute | solution.py:35
  14.6 21.9 %collective-permute-start.4 = (bf16[8,1280]{1,0:T(8,128)(2,1)S(1)}, bf16[8,1280]{1,0:T(8,128)(2,1)S(1)}, u32[]{:S(2)}, u32[]{:S(2)}) collective-permute-start(bf16[8,1280]{1,0:T(8,128)(2,1)S(1)} %get-tuple-element.40), channel_id=1, source_target_pairs={{0,10},{2,12},{4,14},{6,16},{8,18},{10,20},{12,22},{14,24},{16,26}... | collective-permute-start | bytes 61448 | tf_op jit(solution)/shard_map/ppermute | solution.py:35
  32.2 7.5 %collective-permute-start.5 = (bf16[8,1280]{1,0:T(8,128)(2,1)S(1)}, bf16[8,1280]{1,0:T(8,128)(2,1)S(1)}, u32[]{:S(2)}, u32[]{:S(2)}) collective-permute-start(bf16[8,1280]{1,0:T(8,128)(2,1)S(1)} %get-tuple-element.39), channel_id=1, source_target_pairs={{0,12},{2,14},{4,16},{6,18},{8,20},{10,22},{12,24},{14,26},{16,28}... | collective-permute-start | bytes 61448 | tf_op jit(solution)/shard_map/ppermute | solution.py:35
  33.6 6.8 %collective-permute-start.6 = (bf16[8,1280]{1,0:T(8,128)(2,1)S(1)}, bf16[8,1280]{1,0:T(8,128)(2,1)S(1)}, u32[]{:S(2)}, u32[]{:S(2)}) collective-permute-start(bf16[8,1280]{1,0:T(8,128)(2,1)S(1)} %get-tuple-element.38), channel_id=1, source_target_pairs={{0,14},{2,16},{4,18},{6,20},{8,22},{10,24},{12,26},{14,28},{16,30}... | collective-permute-start | bytes 61448 | tf_op jit(solution)/shard_map/ppermute | solution.py:35
  33.6 8.6 %collective-permute-start.7 = (bf16[8,1280]{1,0:T(8,128)(2,1)S(1)}, bf16[8,1280]{1,0:T(8,128)(2,1)S(1)}, u32[]{:S(2)}, u32[]{:S(2)}) collective-permute-start(bf16[8,1280]{1,0:T(8,128)(2,1)S(1)} %get-tuple-element.37), channel_id=1, source_target_pairs={{0,16},{2,18},{4,20},{6,22},{8,24},{10,26},{12,28},{14,30},{16,0},... | collective-permute-start | bytes 61448 | tf_op jit(solution)/shard_map/ppermute | solution.py:35
  34.2 8.5 %collective-permute-start.8 = (bf16[8,1280]{1,0:T(8,128)(2,1)S(1)}, bf16[8,1280]{1,0:T(8,128)(2,1)S(1)}, u32[]{:S(2)}, u32[]{:S(2)}) collective-permute-start(bf16[8,1280]{1,0:T(8,128)(2,1)S(1)} %get-tuple-element.36), channel_id=1, source_target_pairs={{0,18},{2,20},{4,22},{6,24},{8,26},{10,28},{12,30},{14,0},{16,2},{... | collective-permute-start | bytes 61448 | tf_op jit(solution)/shard_map/ppermute | solution.py:35
  36.5 8.6 %collective-permute-start.9 = (bf16[8,1280]{1,0:T(8,128)(2,1)S(1)}, bf16[8,1280]{1,0:T(8,128)(2,1)S(1)}, u32[]{:S(2)}, u32[]{:S(2)}) collective-permute-start(bf16[8,1280]{1,0:T(8,128)(2,1)S(1)} %get-tuple-element.35), channel_id=1, source_target_pairs={{0,20},{2,22},{4,24},{6,26},{8,28},{10,30},{12,0},{14,2},{16,4},{1... | collective-permute-start | bytes 61448 | tf_op jit(solution)/shard_map/ppermute | solution.py:35
  39.8 6.5 %collective-permute-start.10 = (bf16[8,1280]{1,0:T(8,128)(2,1)S(1)}, bf16[8,1280]{1,0:T(8,128)(2,1)S(1)}, u32[]{:S(2)}, u32[]{:S(2)}) collective-permute-start(bf16[8,1280]{1,0:T(8,128)(2,1)S(1)} %get-tuple-element.34), channel_id=1, source_target_pairs={{0,22},{2,24},{4,26},{6,28},{8,30},{10,0},{12,2},{14,4},{16,6},{18... | collective-permute-start | bytes 61448 | tf_op jit(solution)/shard_map/ppermute | solution.py:35
  40.4 5.9 %collective-permute-start.11 = (bf16[8,1280]{1,0:T(8,128)(2,1)S(1)}, bf16[8,1280]{1,0:T(8,128)(2,1)S(1)}, u32[]{:S(2)}, u32[]{:S(2)}) collective-permute-start(bf16[8,1280]{1,0:T(8,128)(2,1)S(1)} %get-tuple-element.33), channel_id=1, source_target_pairs={{0,24},{2,26},{4,28},{6,30},{8,0},{10,2},{12,4},{14,6},{16,8},{18,... | collective-permute-start | bytes 61448 | tf_op jit(solution)/shard_map/ppermute | solution.py:35
  42.2 4.1 %collective-permute-start.12 = (bf16[8,1280]{1,0:T(8,128)(2,1)S(1)}, bf16[8,1280]{1,0:T(8,128)(2,1)S(1)}, u32[]{:S(2)}, u32[]{:S(2)}) collective-permute-start(bf16[8,1280]{1,0:T(8,128)(2,1)S(1)} %get-tuple-element.32), channel_id=1, source_target_pairs={{0,26},{2,28},{4,30},{6,0},{8,2},{10,4},{12,6},{14,8},{16,10},{18,... | collective-permute-start | bytes 61448 | tf_op jit(solution)/shard_map/ppermute | solution.py:35
  42.7 3.8 %collective-permute-start.13 = (bf16[8,1280]{1,0:T(8,128)(2,1)S(1)}, bf16[8,1280]{1,0:T(8,128)(2,1)S(1)}, u32[]{:S(2)}, u32[]{:S(2)}) collective-permute-start(bf16[8,1280]{1,0:T(8,128)(2,1)S(1)} %get-tuple-element.31), channel_id=1, source_target_pairs={{0,28},{2,30},{4,0},{6,2},{8,4},{10,6},{12,8},{14,10},{16,12},{18,... | collective-permute-start | bytes 61448 | tf_op jit(solution)/shard_map/ppermute | solution.py:35
  45.0 2.7 collective-permute-start.14
Sparse Core Ops, SparseCore 0:
  172.6 97.6 reduce-scatter.1
